TPU v7x, 256 devices: a whole 4x4x8 slice. The times are simulated.
256 devices in a mesh: docs: 2 (over y_hi), ctx: 8 (over z), mp: 16 (over y_lo, x, core).
Axes of the slice: x: 4, y: 4 (y_hi: 2, y_lo: 2; y = y_hi * 2 + y_lo), z: 8, core: 2. Of those that a mesh axis runs over, the one named last changes fastest.
Arguments:
- residual_in: bfloat16 [8192, 5376], P(('docs', 'ctx', 'mp')), parts along dimension 0, may hold values from -15 to 15
- document_start: int32 [8192], P(('docs', 'ctx')), parts along dimension 0, may hold values from 0 to 3584, as said below
- input_gain: float32 [5376], replicated, may hold values from 0.25 to 1.75
- query_weight: bfloat16 [5376, 4096], P(None, 'mp'), may hold values from -0.078125 to 0.078125
- key_weight: bfloat16 [5376, 2048], P(None, 'mp'), may hold values from -0.078125 to 0.078125
- value_weight: bfloat16 [5376, 2048], P(None, 'mp'), may hold values from -0.078125 to 0.078125
- query_gain: float32 [128], replicated, may hold values from 0.6 to 20
- key_gain: float32 [128], replicated, may hold values from 0.6 to 20
- output_weight: bfloat16 [4096, 5376], P('mp'), may hold values from -0.09375 to 0.09375
- post_gain: float32 [5376], replicated, may hold values from 0.25 to 1.75
Outputs:
- residual_out: bfloat16 [8192, 5376], P(('docs', 'ctx', 'mp')), parts along dimension 0
There are 2 independent parts, one for each index of `docs`. A program takes and returns all parts, laid end to end along the dimension named above; an argument that names none is the same for every part. Nothing has to cross between parts.
Inputs may be any that keep to these rules, and one draw needn't show every extreme that they name: `document_start`: each entry is the index of the first token of that token's document; the documents lie end to end, there are 4 of them, one has exactly 3072 tokens, and the last has exactly 512 tokens.
All inputs are finite; a program needn't handle non-finite values.
Results may differ from a plain program's by a relative error of at most 0.014.
The roundings to bfloat16 on the way count: a program that leaves them out, or rounds other values in their place, can miss the bound.
Values may be sent and summed in bfloat16 or wider, within the bound.
No kernel may reach another device: no remote copies, remote signals or barrier semaphores. Data moves between devices by JAX's collectives and lax.ppermute only.
A program may use at most 64 MiB of HBM per device.

v0:
```python
import math
import jax
import jax.numpy as jnp
from jax import lax
from jax.sharding import PartitionSpec as P

query_scalar = 168.0
rope_base = 1000000.0
rope_factor = 8.0
epsilon = 1e-06


def make_angles(positions, head_size):
    frequency = rope_base ** (-(jnp.arange(head_size // 2, dtype=jnp.float32) * 2.0 / head_size))
    return (positions.astype(jnp.float32) / rope_factor)[:, None] * frequency[None, :]


def norm_rotate(values, head_gain, angles, head_count):
    tokens_here = values.shape[0]
    head_size = head_gain.shape[0]
    shaped = values.reshape(tokens_here, head_count, head_size)
    scaled = (
        shaped * lax.rsqrt(jnp.mean(shaped * shaped, axis=-1, keepdims=True) + epsilon) * head_gain
    )
    half_size = head_size // 2
    first_half = scaled[..., :half_size]
    second_half = scaled[..., half_size:]
    cosine = jnp.cos(angles)[:, None, :]
    sine_values = jnp.sin(angles)[:, None, :]
    rotated = jnp.concatenate(
        [
            first_half * cosine - second_half * sine_values,
            second_half * cosine + first_half * sine_values,
        ],
        axis=-1,
    )
    return rotated.astype(jnp.bfloat16)


def block_step(query_block, carried, key_piece, value_piece, key_index, first_row, piece_rows):
    queries, query_index, query_start = query_block

    def compute(running):
        running_max, running_total, accumulated = running
        scores = jnp.einsum(
            "tkgd,nkd->tkgn", queries, key_piece, preferred_element_type=jnp.float32
        ) / math.sqrt(query_scalar)
        allowed = (key_index[None, :] >= query_start[:, None]) & (
            key_index[None, :] <= query_index[:, None]
        )
        allowed = allowed[:, None, None, :]
        masked = jnp.where(allowed, scores, -1e30)
        new_max = jnp.maximum(running_max, jnp.max(masked, axis=-1))
        weights = jnp.where(allowed, jnp.exp(masked - new_max[..., None]), 0.0)
        new_total = jnp.sum(weights, axis=-1)
        product = jnp.einsum(
            "tkgn,nkd->tkgd",
            weights.astype(jnp.bfloat16),
            value_piece,
            preferred_element_type=jnp.float32,
        )
        return (new_max, new_total, product)

    def keep(running):
        return running

    is_live = (first_row <= jnp.max(query_index)) & (
        first_row + piece_rows - 1 >= jnp.min(query_start)
    )
    return lax.cond(is_live, compute, keep, carried)


def attend(query_blocks, key_rows, value_rows):
    initial = []
    for query_block in query_blocks:
        query_rows, kv_count, group_size, head_size = query_block[0].shape
        initial.append(
            (
                jnp.full((query_rows, kv_count, group_size), -1e30, jnp.float32),
                jnp.zeros((query_rows, kv_count, group_size), jnp.float32),
                jnp.zeros((query_rows, kv_count, group_size, head_size), jnp.float32),
            )
        )
    carried = tuple(initial)
    first_row = jnp.int32(0)
    key_piece = lax.all_gather(key_rows, "ctx", axis=0, tiled=True)
    value_piece = lax.all_gather(value_rows, "ctx", axis=0, tiled=True)
    piece_rows = key_piece.shape[0]
    key_index = jnp.arange(piece_rows, dtype=jnp.int32)
    outcome = []
    for query_block, carry_block in zip(query_blocks, carried):
        outcome.append(
            block_step(
                query_block, carry_block, key_piece, value_piece, key_index, first_row, piece_rows
            )
        )
    finals = tuple(outcome)
    results = []
    for final_block in finals:
        running_max, running_total, accumulated = final_block
        query_rows = accumulated.shape[0]
        results.append(
            (accumulated / running_total[..., None]).reshape(query_rows, -1).astype(jnp.bfloat16)
        )
    return results[0]


def body(
    residual_in,
    document_start,
    input_gain,
    query_weight,
    key_weight,
    value_weight,
    query_gain,
    key_gain,
    output_weight,
    post_gain,
):
    head_size = query_gain.shape[0]
    gathered = lax.all_gather(residual_in, "mp", axis=0, tiled=True)
    local_tokens = gathered.shape[0]
    widened = gathered.astype(jnp.float32)
    normed = (
        widened
        * lax.rsqrt(jnp.mean(widened * widened, axis=-1, keepdims=True) + epsilon)
        * input_gain
    ).astype(jnp.bfloat16)
    query_raw = jnp.dot(normed, query_weight, preferred_element_type=jnp.float32)
    key_raw = jnp.dot(normed, key_weight, preferred_element_type=jnp.float32)
    value_rows = jnp.dot(normed, value_weight, preferred_element_type=jnp.float32).astype(
        jnp.bfloat16
    )
    query_count = query_weight.shape[1] // head_size
    kv_count = key_weight.shape[1] // head_size
    group_size = query_count // kv_count
    block_index = lax.axis_index("ctx")
    positions = block_index * local_tokens + jnp.arange(local_tokens, dtype=jnp.int32)
    angles = make_angles(positions - document_start, head_size)
    query_rot = norm_rotate(query_raw, query_gain, angles, query_count).reshape(
        local_tokens, kv_count, group_size, head_size
    )
    key_rot = norm_rotate(key_raw, key_gain, angles, kv_count)
    value_heads = value_rows.reshape(local_tokens, kv_count, head_size)
    attended = attend([(query_rot, positions, document_start)], key_rot, value_heads)
    summed = lax.psum_scatter(
        jnp.dot(attended, output_weight, preferred_element_type=jnp.float32).astype(jnp.bfloat16),
        "mp",
        scatter_dimension=0,
        tiled=True,
    ).astype(jnp.float32)
    branch = (
        summed * lax.rsqrt(jnp.mean(summed * summed, axis=-1, keepdims=True) + epsilon) * post_gain
    )
    return (residual_in.astype(jnp.float32) + branch).astype(jnp.bfloat16)


def solution(mesh):
    return jax.shard_map(
        body,
        mesh=mesh,
        in_specs=(
            P(("docs", "ctx", "mp"), None),
            P(("docs", "ctx")),
            P(),
            P(None, "mp"),
            P(None, "mp"),
            P(None, "mp"),
            P(),
            P(),
            P("mp", None),
            P(),
        ),
        out_specs=P(("docs", "ctx", "mp"), None),
        check_vma=False,
    )
```

profile of v0, /device:TPU:32, one launch (start us, length us, event | category | flops | bytes accessed | tf_op | source)
XLA Modules:
  0.0 245.3 jit_solution(6276417553406046301)
XLA Ops:
  6.5 0.0 copy-start
  6.5 0.0 copy-start.5
  6.5 0.0 all-gather.5.cloned.1.call-start
  6.5 0.7 all-gather.5.cloned.1.call-update
  7.3 0.0 all-gather.9.cloned.1.call-start
  7.3 47.2 %all-gather.5.cloned.1.call-done = bf16[512,5376]{1,0:T(8,128)(2,1)} async-done(((bf16[32,5376]{1,0:T(8,128)(2,1)}), bf16[512,5376]{1,0:T(8,128)(2,1)}) %all-gather.5.cloned.1.call-update) | async-done | bytes 5505040 | tf_op jit(solution)/shard_map/all_gather | solution.py:121
  54.5 0.0 copy-start.2
  54.5 3.9 %fusion.17 = f32[512]{0:T(512)S(1)} fusion(bf16[512,5376]{1,0:T(8,128)(2,1)} %all-gather.5.cloned.1.call-done), kind=kLoop, calls=%fused_computation.20 | loop fusion | flops 8257024 | bytes 5507072 | tf_op jit(solution)/shard_map/reduce_sum | solution.py:126
  58.3 0.0 copy-done.5
  58.3 0.3 copy-done.2
  58.6 0.0 copy-start.9
  58.6 1.9 fusion.19
  60.5 0.0 copy-start.1
  60.5 2.4 copy-done.1
  62.9 0.0 copy-done.9
  62.9 0.0 copy-start.6
  62.9 2.3 convolution_convert_fusion.1
  65.2 0.0 copy-start.7
  65.2 0.0 all-gather.9.cloned.1.call-update
  65.2 0.0 all-gather.7.cloned.1.call-start
  65.3 0.0 copy-done.6
  65.3 4.9 %multiply_reduce_fusion.1 = (f32[512]{0:T(512)S(1)}, f32[512,128]{0,1:T(8,128)S(1)}) fusion(bf16[512,5376]{1,0:T(8,128)(2,1)} %copy-done.1, bf16[5376,128]{1,0:T(8,128)(2,1)} %param.16), kind=kOutput, calls=%fused_computation.42 | convolution fusion | flops 704773632 | bytes 7145472 | tf_op jit(solution)/shard_map/dot_general | solution.py:130
  70.3 0.0 copy-done.7
  70.3 0.1 multiply_bitcast_fusion
  70.4 0.6 fusion.31
  70.9 0.7 pad_maximum_fusion.1
  71.6 0.0 all-gather.7.cloned.1.call-update
  71.6 0.0 reduce-scatter.2.cloned.1.call-start
  71.7 0.6 fusion.34
  72.3 0.7 reduce_min.9
  74.3 0.6 iota_add_fusion
  74.9 1.7 multiply_cosine_fusion
  76.6 0.0 copy-start.8
  76.6 5.9 %multiply_reduce_fusion = (f32[512,2]{0,1:T(2,128)S(1)}, f32[512,256]{0,1:T(8,128)}) fusion(bf16[512,5376]{1,0:T(8,128)(2,1)} %copy-done.1, bf16[5376,256]{1,0:T(8,128)(2,1)} %param.15), kind=kOutput, calls=%fused_computation.35 | convolution fusion | flops 1409547264 | bytes 8785920 | tf_op jit(solution)/shard_map/dot_general | solution.py:129
  82.5 1.2 copy.21
  83.7 0.0 copy-done.8
  83.7 0.2 multiply_multiply_fusion
  83.9 1.2 fusion.24
  85.1 0.1 pad_maximum_fusion
  85.3 17.8 %all-gather.9.cloned.1.call-done = bf16[4096,128]{1,0:T(8,128)(2,1)} async-done(((bf16[512,128]{1,0:T(8,128)(2,1)}), bf16[4096,128]{1,0:T(8,128)(2,1)}) %all-gather.9.cloned.1.call-update) | async-done | bytes 1048592 | tf_op jit(solution)/shard_map/all_gather | solution.py:87
  103.1 39.0 %all-gather.7.cloned.1.call-done = bf16[4096,1,128]{0,2,1:T(8,128)(2,1)} async-done(((bf16[512,1,128]{0,2,1:T(8,128)(2,1)}), bf16[4096,1,128]{0,2,1:T(8,128)(2,1)}) %all-gather.7.cloned.1.call-update) | async-done | bytes 1048592 | tf_op jit(solution)/shard_map/all_gather | solution.py:86
  142.2 18.4 %conditional.1 = (f32[512,1,2]{0,2,1:T(2,128)S(1)}, f32[512,1,2,128]{0,3,2,1:T(8,128)S(1)}) conditional(s32[]{:T(128)} %convert_element_type.54, () %tuple.13, (s32[4096]{0:T(1024)S(1)}, s32[4096]{0:T(1024)S(1)}, s32[512]{0:T(512)}, s32[512]{0:T(512)}, bf16[4096,1,128]{0,2,1:T(8,128)(2,1)}, /*index=5*/bf16[512,1,2,128]{3,0,2,1:T(8,128)(2,1)S(1)}, ...), branch_computations={%region_5.0_spmd, %region_6.9_spmd} | conditional | flops 2208300032 | bytes 65859628 | solution.py:70
  142.2 3.8 %compare_and_fusion = pred[512,4096]{0,1:T(8,128)(4,1)S(1)} fusion(s32[512]{0:T(512)} %get-tuple-element.21, s32[512]{0:T(512)} %get-tuple-element.19, s32[4096]{0:T(1024)S(1)} %get-tuple-element.20, s32[4096]{0:T(1024)S(1)} %get-tuple-element.20), kind=kLoop, calls=%fused_computation.8 | loop fusion | flops 6291456 | bytes 2134016 | tf_op jit(solution)/shard_map/cond/branch_1_fun/and | solution.py:48
  146.0 0.0 copy-start.10
  146.0 5.2 %fusion = (f32[512,2]{0,1:T(2,128)S(1)}, f32[4096,512,2]{1,0,2:T(8,128)S(1)}) fusion(pred[512,4096]{0,1:T(8,128)(4,1)S(1)} %compare_and_fusion, bf16[512,1,2,128]{3,0,2,1:T(8,128)(2,1)S(1)} %get-tuple-element.23, bf16[4096,1,128]{0,2,1:T(8,128)(2,1)} %get-tuple-element.47), kind=kOutput, calls=%fused_computation.2 | convolution fusion | flops 1086323712 | bytes 20189184 | tf_op jit(solution)/shard_map/cond/branch_1_fun/tkgd,nkd->tkgn/dot_general | solution.py:45
  151.2 0.0 copy-done.10
  151.2 5.0 %fusion.7 = f32[512,1,2,128]{0,3,2,1:T(8,128)S(1)} fusion(f32[4096,512,2]{1,0,2:T(8,128)S(1)} %get-tuple-element.52, f32[512,2]{0,1:T(2,128)S(1)} %broadcast_maximum_fusion, pred[512,4096]{0,1:T(8,128)(4,1)S(1)} %compare_and_fusion, bf16[4096,1,128]{2,0,1:T(8,128)(2,1)S(1)} %copy-done.10), kind=kOutput, calls=%fused_computation.9 | convolution fusion | flops 1094713344 | bytes 20451328 | tf_op jit(solution)/shard_map/cond/branch_1_fun/tkgn,nkd->tkgd/dot_general | solution.py:56
  156.1 4.4 %fusion.2 = f32[512,2]{0,1:T(2,128)S(1)} fusion(f32[4096,512,2]{1,0,2:T(8,128)S(1)} %get-tuple-element.52, f32[512,2]{0,1:T(2,128)S(1)} %broadcast_maximum_fusion, pred[512,4096]{0,1:T(8,128)(4,1)S(1)} %compare_and_fusion), kind=kLoop, calls=%fused_computation.4 | loop fusion | flops 20970496 | bytes 18882560 | tf_op jit(solution)/shard_map/cond/branch_1_fun/reduce_sum | solution.py:55
  160.6 0.1 divide_convert_fusion
  160.7 0.0 copy-done
  160.7 0.0 copy-start.3
  160.7 0.0 copy-start.4
  160.7 4.0 %convolution_convert_fusion = bf16[512,5376]{1,0:T(8,128)(2,1)} fusion(bf16[512,256]{0,1:T(8,128)(2,1)S(1)} %bitcast.65, bf16[256,5376]{1,0:T(8,128)(2,1)S(1)} %copy-done), kind=kOutput, calls=%fused_computation.23 | convolution fusion | flops 1412038656 | bytes 8519680 | tf_op jit(solution)/shard_map/dot_general | solution.py:147
  164.7 0.0 reduce-scatter.2.cloned.1.call-update
  164.8 70.9 %reduce-scatter.2.cloned.1.call-done = bf16[32,5376]{1,0:T(8,128)(2,1)} async-done(((bf16[512,5376]{1,0:T(8,128)(2,1)}), bf16[32,5376]{1,0:T(8,128)(2,1)}) %reduce-scatter.2.cloned.1.call-update) | async-done | bytes 344080 | tf_op jit(solution)/shard_map/reduce_scatter | solution.py:146
  235.7 1.2 fusion.20
  236.8 0.0 copy-done.3
  236.9 0.0 copy-done.4
  236.9 1.9 fusion.23
  (8 shorter events, 0.1 us)
Async XLA Ops:
  6.5 154.1 %copy-start = (bf16[256,5376]{1,0:T(8,128)(2,1)S(1)}, bf16[256,5376]{1,0:T(8,128)(2,1)}, u32[]{:S(2)}) copy-start(bf16[256,5376]{1,0:T(8,128)(2,1)} %param.20) | copy-start | bytes 8257540
  6.5 51.8 %copy-start.5 = (f32[5376]{0:T(1024)S(1)}, f32[5376]{0:T(1024)}, u32[]{:S(2)}) copy-start(f32[5376]{0:T(1024)} %param.14) | copy-start | bytes 64516
  6.5 47.9 %all-gather.5.cloned.1.call-start = ((), (), s32[]{:S(2)}) async-start(), calls=%async_computation.1 | async-start | bytes 5849088 | tf_op jit(solution)/shard_map/all_gather | solution.py:121
  7.3 95.9 %all-gather.9.cloned.1.call-start = ((), (), s32[]{:S(2)}) async-start(), calls=%async_computation.4 | async-start | bytes 1179648 | tf_op jit(solution)/shard_map/all_gather | solution.py:87
  54.5 4.2 %copy-start.2 = (bf16[512,5376]{1,0:T(8,128)(2,1)S(1)}, bf16[512,5376]{1,0:T(8,128)(2,1)}, u32[]{:S(2)}) copy-start(bf16[512,5376]{1,0:T(8,128)(2,1)} %all-gather.5.cloned.1.call-done) | copy-start | bytes 16515076
  58.6 4.3 %copy-start.9 = (bf16[5376,128]{1,0:T(8,128)(2,1)S(1)}, bf16[5376,128]{1,0:T(8,128)(2,1)}, u32[]{:S(2)}) copy-start(bf16[5376,128]{1,0:T(8,128)(2,1)} %param.17) | copy-start | bytes 4128772
  60.5 2.4 copy-start.1
  62.9 2.4 copy-start.6
  65.2 5.1 %copy-start.7 = (f32[128]{0:T(128)S(1)}, f32[128]{0:T(128)}, u32[]{:S(2)}) copy-start(f32[128]{0:T(128)} %param.19) | copy-start | bytes 1540
  65.2 77.0 %all-gather.7.cloned.1.call-start = ((), (), s32[]{:S(2)}) async-start(), calls=%async_computation.2 | async-start | bytes 1179648 | tf_op jit(solution)/shard_map/all_gather | solution.py:86
  71.6 164.1 %reduce-scatter.2.cloned.1.call-start = ((), (), s32[]{:S(2)}) async-start(), calls=%async_computation.3 | async-start | bytes 5849088 | tf_op jit(solution)/shard_map/reduce_scatter | solution.py:146
  76.6 7.1 %copy-start.8 = (f32[128]{0:T(128)S(1)}, f32[128]{0:T(128)}, u32[]{:S(2)}) copy-start(f32[128]{0:T(128)} %param.18) | copy-start | bytes 1540
  146.0 5.2 %copy-start.10 = (bf16[4096,1,128]{2,0,1:T(8,128)(2,1)S(1)}, bf16[4096,1,128]{2,0,1:T(8,128)(2,1)}, u32[]{:S(2)}) copy-start(bf16[4096,1,128]{2,0,1:T(8,128)(2,1)} %get-tuple-element.24) | copy-start | bytes 3145732 | tf_op jit(solution)/shard_map/cond
  160.7 76.2 %copy-start.3 = (bf16[32,5376]{1,0:T(8,128)(2,1)S(1)}, bf16[32,5376]{1,0:T(8,128)(2,1)}, u32[]{:S(2)}) copy-start(bf16[32,5376]{1,0:T(8,128)(2,1)} %param.12) | copy-start | bytes 1032196
  160.7 76.2 %copy-start.4 = (f32[5376]{0:T(1024)S(1)}, f32[5376]{0:T(1024)}, u32[]{:S(2)}) copy-start(f32[5376]{0:T(1024)} %param.21) | copy-start | bytes 64516
Sparse Core Ops, SparseCore 0:
  9.2 45.2 all-gather.4
  65.3 37.7 all-gather.8
  104.9 37.1 all-gather.6
  164.9 70.7 reduce-scatter.1
where the time goes:
time: 246 us; the launch traced here: 245 us
  waiting for transfers between devices  176 us (72%)
  matrix products  27.2 us (11%)
  other arithmetic  23.6 us (10%)
  between operations  14.6 us (6%)
  local copies, waits for them, and re-layouts  3.97 us (2%)
    reduce_scatter x1, waiting for transfers between devices, body(): lax.psum_scatter(jnp.dot(attended, output_weight, preferred_element_type=...  70.9 us
    all_gather x1, waiting for transfers between devices, body(): gathered = lax.all_gather(residual_in, 'mp', axis=0, tiled=True)  47.2 us
    all_gather x1, waiting for transfers between devices, attend(): key_piece = lax.all_gather(key_rows, 'ctx', axis=0, tiled=True)  39 us
    all_gather x1, waiting for transfers between devices, attend(): value_piece = lax.all_gather(value_rows, 'ctx', axis=0, tiled=True)  17.8 us
    dot_general x1, matrix products, body(): jnp.dot(normed, query_weight, preferred_element_type=jnp.float32)  5.87 us
    dot_general x1, matrix products, compute(): jnp.einsum('tkgd,nkd->tkgn', queries, key_piece, preferred_element_type=j...  5.17 us
    dot_general x1, matrix products, compute(): jnp.einsum('tkgn,nkd->tkgd', weights.astype(jnp.bfloat16), value_piece, p...  4.97 us
    dot_general x1, matrix products, body(): key_raw = jnp.dot(normed, key_weight, preferred_element_type=jnp.float32)  4.92 us
  transfers between devices with their start and end apart: 4, of which 4 were waited for; matrix products, arithmetic and copies ran while one was open for 8% of the time, Pallas kernels for 0%

commit v1 on v0

--- a/solution.py
+++ b/solution.py
@@ -83,7 +83,20 @@
         )
     carried = tuple(initial)
     first_row = jnp.int32(0)
-    key_piece = lax.all_gather(key_rows, "ctx", axis=0, tiled=True)
+    n_axis = lax.psum(1, "ctx")
+    slots = [(tick, (tick + 1) % n_axis) for tick in range(n_axis)]
+    kept_rows = [(tick, (tick - 1) % n_axis) for tick in range(n_axis)]
+    low, small = ([key_rows], [key_rows])
+    for _ in range(n_axis // 2):
+        d_next = lax.ppermute(low[-1], "ctx", perm=slots)
+        low.append(d_next)
+    for _ in [*range((n_axis - 1) // 2)]:
+        small.append(lax.ppermute(small[-1], "ctx", perm=kept_rows))
+    key_piece = jnp.roll(
+        jnp.concatenate([*low[::-1], *small[1:]], 0),
+        (lax.axis_index("ctx") - n_axis // 2) * key_rows.shape[0],
+        0,
+    )
     value_piece = lax.all_gather(value_rows, "ctx", axis=0, tiled=True)
     piece_rows = key_piece.shape[0]
     key_index = jnp.arange(piece_rows, dtype=jnp.int32)

time: 246 us -> 222 us (0.902)
  waiting for transfers between devices: 176 us -> 126 us
  local copies, waits for them, and re-layouts: 3.97 us -> 16.9 us
  starting transfers between devices: 0.13 us -> 9.77 us
  other arithmetic: 23.6 us -> 29.6 us
  matrix products: 27.2 us -> 24.5 us
    all_gather x1 -> x0, waiting for transfers between devices: 39 us -> none  [attend(): key_piece = lax.all_gather(key_rows, 'ctx', axis=0, tiled=True)]
    all_gather x1, waiting for transfers between devices: 17.8 us -> 0.01 us  [attend(): value_piece = lax.all_gather(value_rows, 'ctx', axis=0, tiled=True)]
    ppermute x0 -> x7, waiting for transfers between devices: none -> 10.7 us  [the longest x4 10.7 us: attend(): d_next = lax.ppermute(low[-1], 'ctx', perm=slots)]
    ppermute x0 -> x7, starting transfers between devices: none -> 9.68 us  [the longest x4 8.12 us: attend(): d_next = lax.ppermute(low[-1], 'ctx', perm=slots)]
    unnamed x20 -> x33, local copies, waits for them, and re-layouts: 2.73 us -> 10.9 us
    all_gather x1, waiting for transfers between devices: 47.2 us -> 40.8 us  [body(): gathered = lax.all_gather(residual_in, 'mp', axis=0, tiled=True)]
    another operation x0 -> x1, local copies, waits for them, and re-layouts: none -> 4.06 us
    dot_general x1, matrix products: 4.92 us -> 1.96 us  [body(): key_raw = jnp.dot(normed, key_weight, preferred_element_type=jnp.float32)]
  transfers between devices with their start and end apart: 4 -> 10, of which waited for: 4 -> 5; matrix products, arithmetic and copies ran while one was open for 8% -> 13% of each run, Pallas kernels for 0% -> 0%
where the time goes in v1:
time: 222 us; the launch traced here: 221 us
  waiting for transfers between devices  126 us (57%)
  other arithmetic  29.6 us (13%)
  matrix products  24.5 us (11%)
  local copies, waits for them, and re-layouts  16.9 us (8%)
  between operations  14.6 us (7%)
  starting transfers between devices  9.77 us (4%)
    reduce_scatter x1, waiting for transfers between devices, body(): lax.psum_scatter(jnp.dot(attended, output_weight, preferred_element_type=...  73.5 us
    all_gather x1, waiting for transfers between devices, body(): gathered = lax.all_gather(residual_in, 'mp', axis=0, tiled=True)  40.8 us
    unnamed x33, local copies, waits for them, and re-layouts  10.9 us
    ppermute x4, waiting for transfers between devices, attend(): d_next = lax.ppermute(low[-1], 'ctx', perm=slots)  10.7 us
    ppermute x4, starting transfers between devices, attend(): d_next = lax.ppermute(low[-1], 'ctx', perm=slots)  8.12 us
    dot_general x1, matrix products, body(): jnp.dot(normed, query_weight, preferred_element_type=jnp.float32)  5.85 us
    dot_general x1, matrix products, compute(): jnp.einsum('tkgd,nkd->tkgn', queries, key_piece, preferred_element_type=j...  5.42 us
    reduce_sum x1, other arithmetic, compute(): new_total = jnp.sum(weights, axis=-1)  5.04 us
  transfers between devices with their start and end apart: 10, of which 5 were waited for; matrix products, arithmetic and copies ran while one was open for 13% of the time, Pallas kernels for 0%

profile of v1, /device:TPU:32, one launch (start us, length us, event | category | flops | bytes accessed | tf_op | source)
XLA Modules:
  0.0 221.1 jit_solution(4326394822888449590)
XLA Ops:
  6.5 0.7 all-gather.4.cloned.1.call-update
  7.3 0.0 all-gather.6.cloned.1.call-start
  7.3 0.6 fusion.36
  8.6 1.3 reduce_min.9
  10.6 0.6 iota_add_fusion
  11.2 0.7 convert_multiply_fusion.4
  11.9 1.8 multiply_cosine_fusion
  13.7 40.8 %all-gather.4.cloned.1.call-done = bf16[512,5376]{1,0:T(8,128)(2,1)} async-done(((bf16[32,5376]{1,0:T(8,128)(2,1)}), bf16[512,5376]{1,0:T(8,128)(2,1)}) %all-gather.4.cloned.1.call-update) | async-done | bytes 5505040 | tf_op jit(solution)/shard_map/all_gather | solution.py:134
  54.5 3.9 %fusion.19 = f32[512]{0:T(512)S(1)} fusion(bf16[512,5376]{1,0:T(8,128)(2,1)} %all-gather.4.cloned.1.call-done), kind=kLoop, calls=%fused_computation.22 | loop fusion | flops 8257024 | bytes 5507072 | tf_op jit(solution)/shard_map/reduce_sum | solution.py:139
  58.3 0.3 copy-done.2
  58.6 1.9 fusion.21
  60.5 0.0 copy-start.9
  60.6 0.0 copy-start.11
  60.6 2.0 multiply_reduce_fusion.1
  62.6 0.1 multiply_bitcast_fusion
  62.6 0.6 fusion.33
  63.2 0.7 pad_maximum_fusion.1
  63.9 0.5 collective-permute-start.4
  64.3 1.6 collective-permute-start
  65.9 2.2 %convolution_convert_fusion.1 = bf16[512,128]{1,0:T(8,128)(2,1)} fusion(bf16[512,5376]{1,0:T(8,128)(2,1)S(1)} %fusion.21, bf16[5376,128]{1,0:T(8,128)(2,1)S(1)} %copy-done.11), kind=kOutput, calls=%fused_computation.26 | convolution fusion | flops 704708608 | bytes 7012352 | tf_op jit(solution)/shard_map/dot_general | solution.py:144
  68.1 0.0 all-gather.6.cloned.1.call-update
  68.2 0.0 copy-start.10
  68.2 0.0 reduce-scatter.2.cloned.1.call-start
  68.2 5.9 %multiply_reduce_fusion = (f32[512,2]{0,1:T(2,128)S(1)}, f32[512,256]{0,1:T(8,128)}) fusion(bf16[512,5376]{1,0:T(8,128)(2,1)} %copy-done.1, bf16[5376,256]{1,0:T(8,128)(2,1)} %param.15), kind=kOutput, calls=%fused_computation.37 | convolution fusion | flops 1409547264 | bytes 8785920 | tf_op jit(solution)/shard_map/dot_general | solution.py:142
  74.1 1.2 copy.21
  75.3 1.6 collective-permute-start.1
  77.0 5.4 %collective-permute-done.1 = bf16[512,1,128]{0,2,1:T(8,128)(2,1)S(1)} collective-permute-done((bf16[512,1,128]{0,2,1:T(8,128)(2,1)}, bf16[512,1,128]{0,2,1:T(8,128)(2,1)S(1)}, u32[]{:S(2)}, u32[]{:S(2)}) %collective-permute-start.1) | collective-permute-done | bytes 131104 | tf_op jit(solution)/shard_map/ppermute | solution.py:91
  82.4 2.5 %collective-permute-start.2 = (bf16[512,1,128]{0,2,1:T(8,128)(2,1)S(1)}, bf16[512,1,128]{0,2,1:T(8,128)(2,1)S(1)}, u32[]{:S(2)}, u32[]{:S(2)}) collective-permute-start(bf16[512,1,128]{0,2,1:T(8,128)(2,1)S(1)} %collective-permute-done.1), channel_id=1, source_target_pairs={{0,16},{16,32},{32,48},{48,64},{64,80},{80,96},{96,112},{112,0},{1... | collective-permute-start | bytes 393224 | tf_op jit(solution)/shard_map/ppermute | solution.py:91
  84.9 0.2 multiply_multiply_fusion
  85.1 0.4 collective-permute-start.5
  85.5 3.4 %collective-permute-done.2 = bf16[512,1,128]{0,2,1:T(8,128)(2,1)S(1)} collective-permute-done((bf16[512,1,128]{0,2,1:T(8,128)(2,1)S(1)}, bf16[512,1,128]{0,2,1:T(8,128)(2,1)S(1)}, u32[]{:S(2)}, u32[]{:S(2)}) %collective-permute-start.2) | collective-permute-done | bytes 131104 | tf_op jit(solution)/shard_map/ppermute | solution.py:91
  88.8 2.5 %collective-permute-start.3 = (bf16[512,1,128]{0,2,1:T(8,128)(2,1)S(1)}, bf16[512,1,128]{0,2,1:T(8,128)(2,1)S(1)}, u32[]{:S(2)}, u32[]{:S(2)}) collective-permute-start(bf16[512,1,128]{0,2,1:T(8,128)(2,1)S(1)} %collective-permute-done.2), channel_id=1, source_target_pairs={{0,16},{16,32},{32,48},{48,64},{64,80},{80,96},{96,112},{112,0},{1... | collective-permute-start | bytes 393224 | tf_op jit(solution)/shard_map/ppermute | solution.py:91
  91.3 1.3 fusion.26
  92.6 0.9 pad_maximum_fusion
  93.4 0.7 collective-permute-start.6
  94.1 1.9 collective-permute-done.3
  96.0 0.7 constant_dynamic-update-slice_fusion.15
  96.7 0.7 constant_dynamic-update-slice_fusion.14
  97.4 0.7 constant_dynamic-update-slice_fusion.13
  98.0 1.6 constant_dynamic-update-slice_fusion.12
  99.6 0.7 constant_dynamic-update-slice_fusion.11
  100.3 0.7 constant_dynamic-update-slice_fusion.10
  101.0 0.7 constant_dynamic-update-slice_fusion.9
  101.6 0.7 constant_dynamic-update-slice_fusion.8
  102.3 0.7 constant_dynamic-update-slice_fusion.7
  103.0 0.7 constant_dynamic-update-slice_fusion.6
  103.7 0.7 constant_dynamic-update-slice_fusion.5
  104.4 1.6 constant_dynamic-update-slice_fusion.4
  105.9 0.7 constant_dynamic-update-slice_fusion.3
  106.6 0.7 constant_dynamic-update-slice_fusion.2
  107.3 0.7 constant_dynamic-update-slice_fusion.1
  108.0 0.7 constant_dynamic-update-slice_fusion
  108.7 24.6 %conditional.1 = (f32[512,1,2]{0,2,1:T(2,128)}, f32[512,1,2,128]{0,3,2,1:T(8,128)S(1)}) conditional(s32[]{:T(128)} %convert_element_type.57, () %tuple.24, (s32[4096]{0:T(1024)S(1)}, s32[4096]{0:T(1024)S(1)}, s32[512]{0:T(512)}, s32[512]{0:T(512)}, s32[]{:T(128)}, /*index=5*/s32[]{:T(128)}, bf16[8192,1,128]{0,2,1:T(8,128)(2,1)}, ...), branch_computations={%region_5.6_spmd, %region_6.9_spmd} | conditional | flops 2208300032 | bytes 79491328 | solution.py:70
  108.7 5.0 %compare_and_fusion = pred[512,4096]{0,1:T(8,128)(4,1)} fusion(s32[512]{0:T(512)} %get-tuple-element.118, s32[512]{0:T(512)} %get-tuple-element.116, s32[4096]{0:T(1024)S(1)} %get-tuple-element.117, s32[4096]{0:T(1024)S(1)} %get-tuple-element.117), kind=kLoop, calls=%fused_computation.8 | loop fusion | flops 6291456 | bytes 2134016 | tf_op jit(solution)/shard_map/cond/branch_1_fun/and | solution.py:48
  113.7 4.1 %copy.22 = bf16[8192,1,128]{2,0,1:T(8,128)(2,1)} copy(bf16[8192,1,128]{0,2,1:T(8,128)(2,1)} %get-tuple-element.164) | data formatting | bytes 4194304 | tf_op jit(solution)/shard_map
  117.8 5.4 %fusion = (f32[512,2]{0,1:T(2,128)S(1)}, f32[4096,512,2]{1,0,2:T(8,128)S(1)}) fusion(pred[512,4096]{0,1:T(8,128)(4,1)} %compare_and_fusion, bf16[512,1,2,128]{3,0,2,1:T(8,128)(2,1)S(1)} %copy-done.6, bf16[8192,1,128]{2,0,1:T(8,128)(2,1)} %copy.22, s32[]{:T(128)S(6)} %select_n.30), kind=kOutput, calls=%fused_computation.2 | convolution fusion | flops 1086323712 | bytes 20189188 | tf_op jit(solution)/shard_map/cond/branch_1_fun/tkgd,nkd->tkgn/dot_general | solution.py:45
  123.2 5.0 %fusion.7 = f32[512,1,2,128]{0,3,2,1:T(8,128)S(1)} fusion(f32[4096,512,2]{1,0,2:T(8,128)S(1)} %get-tuple-element.174, f32[512,2]{0,1:T(2,128)S(1)} %broadcast_maximum_fusion, pred[512,4096]{0,1:T(8,128)(4,1)S(1)} %copy-done.3, bf16[4096,1,128]{2,0,1:T(8,128)(2,1)S(1)} %copy-done.12), kind=kOutput, calls=%fused_computation.9 | convolution fusion | flops 1094713344 | bytes 20451328 | tf_op jit(solution)/shard_map/cond/branch_1_fun/tkgn,nkd->tkgd/dot_general | solution.py:56
  128.2 5.0 %fusion.2 = f32[512,2]{0,1:T(2,128)} fusion(f32[4096,512,2]{1,0,2:T(8,128)S(1)} %get-tuple-element.174, f32[512,2]{0,1:T(2,128)S(1)} %broadcast_maximum_fusion, pred[512,4096]{0,1:T(8,128)(4,1)S(1)} %copy-done.3), kind=kLoop, calls=%fused_computation.4 | loop fusion | flops 20970496 | bytes 18882560 | tf_op jit(solution)/shard_map/cond/branch_1_fun/reduce_sum | solution.py:55
  133.3 0.7 divide_convert_fusion
  134.0 4.1 %convolution_convert_fusion = bf16[512,5376]{1,0:T(8,128)(2,1)} fusion(bf16[512,256]{0,1:T(8,128)(2,1)S(1)} %bitcast.64, bf16[256,5376]{1,0:T(8,128)(2,1)S(1)} %copy-done), kind=kOutput, calls=%fused_computation.25 | convolution fusion | flops 1412038656 | bytes 8519680 | tf_op jit(solution)/shard_map/dot_general | solution.py:160
  138.1 0.0 reduce-scatter.2.cloned.1.call-update
  138.1 73.5 %reduce-scatter.2.cloned.1.call-done = bf16[32,5376]{1,0:T(8,128)(2,1)} async-done(((bf16[512,5376]{1,0:T(8,128)(2,1)}), bf16[32,5376]{1,0:T(8,128)(2,1)}) %reduce-scatter.2.cloned.1.call-update) | async-done | bytes 344080 | tf_op jit(solution)/shard_map/reduce_scatter | solution.py:159
  211.5 1.2 fusion.22
  212.7 1.9 fusion.25
  (35 shorter events, 0.1 us)
Async XLA Ops:
  6.5 127.4 %copy-start = (bf16[256,5376]{1,0:T(8,128)(2,1)S(1)}, bf16[256,5376]{1,0:T(8,128)(2,1)}, u32[]{:S(2)}) copy-start(bf16[256,5376]{1,0:T(8,128)(2,1)} %param.20) | copy-start | bytes 8257540
  6.5 47.9 %all-gather.4.cloned.1.call-start = ((), (), s32[]{:S(2)}) async-start(), calls=%async_computation.1 | async-start | bytes 5849088 | tf_op jit(solution)/shard_map/all_gather | solution.py:134
  7.3 101.4 %all-gather.6.cloned.1.call-start = ((), (), s32[]{:S(2)}) async-start(), calls=%async_computation.3 | async-start | bytes 1179648 | tf_op jit(solution)/shard_map/all_gather | solution.py:100
  11.9 46.5 %copy-start.8 = (f32[5376]{0:T(1024)S(1)}, f32[5376]{0:T(1024)}, u32[]{:S(2)}) copy-start(f32[5376]{0:T(1024)} %param.14) | copy-start | bytes 64516
  54.5 4.2 %copy-start.2 = (bf16[512,5376]{1,0:T(8,128)(2,1)S(1)}, bf16[512,5376]{1,0:T(8,128)(2,1)}, u32[]{:S(2)}) copy-start(bf16[512,5376]{1,0:T(8,128)(2,1)} %all-gather.4.cloned.1.call-done) | copy-start | bytes 16515076
  58.6 1.9 copy-start.5
  60.5 5.4 %copy-start.1 = (bf16[512,5376]{1,0:T(8,128)(2,1)}, bf16[512,5376]{1,0:T(8,128)(2,1)S(1)}, u32[]{:S(2)}) copy-start(bf16[512,5376]{1,0:T(8,128)(2,1)S(1)} %fusion.21) | copy-start | bytes 16515076
  60.5 2.0 copy-start.9
  60.6 5.3 %copy-start.11 = (bf16[5376,128]{1,0:T(8,128)(2,1)S(1)}, bf16[5376,128]{1,0:T(8,128)(2,1)}, u32[]{:S(2)}) copy-start(bf16[5376,128]{1,0:T(8,128)(2,1)} %param.17) | copy-start | bytes 4128772
  63.9 21.2 %collective-permute-start.4 = (bf16[512,1,128]{0,2,1:T(8,128)(2,1)}, bf16[512,1,128]{0,2,1:T(8,128)(2,1)S(1)}, u32[]{:S(2)}, u32[]{:S(2)}) collective-permute-start(bf16[512,1,128]{0,2,1:T(8,128)(2,1)} %pad_maximum_fusion.1), channel_id=1, source_target_pairs={{0,112},{16,0},{32,16},{48,32},{64,48},{80,64},{96,80},{112,96},{1... | collective-permute-start | bytes 393224 | tf_op jit(solution)/shard_map/ppermute | solution.py:94
  64.3 11.0 %collective-permute-start = (bf16[512,1,128]{0,2,1:T(8,128)(2,1)}, bf16[512,1,128]{0,2,1:T(8,128)(2,1)}, u32[]{:S(2)}, u32[]{:S(2)}) collective-permute-start(bf16[512,1,128]{0,2,1:T(8,128)(2,1)} %pad_maximum_fusion.1), channel_id=1, source_target_pairs={{0,16},{16,32},{32,48},{48,64},{64,80},{80,96},{96,112},{112,0},{1... | collective-permute-start | bytes 393224 | tf_op jit(solution)/shard_map/ppermute | solution.py:91
  68.2 16.7 %copy-start.10 = (f32[128]{0:T(128)S(1)}, f32[128]{0:T(128)}, u32[]{:S(2)}) copy-start(f32[128]{0:T(128)} %param.18) | copy-start | bytes 1540
  68.2 143.4 %reduce-scatter.2.cloned.1.call-start = ((), (), s32[]{:S(2)}) async-start(), calls=%async_computation.2 | async-start | bytes 5849088 | tf_op jit(solution)/shard_map/reduce_scatter | solution.py:159
  75.3 7.1 %collective-permute-start.1 = (bf16[512,1,128]{0,2,1:T(8,128)(2,1)}, bf16[512,1,128]{0,2,1:T(8,128)(2,1)S(1)}, u32[]{:S(2)}, u32[]{:S(2)}) collective-permute-start(bf16[512,1,128]{0,2,1:T(8,128)(2,1)} %collective-permute-done), channel_id=1, source_target_pairs={{0,16},{16,32},{32,48},{48,64},{64,80},{80,96},{96,112},{112,0},{1... | collective-permute-start | bytes 393224 | tf_op jit(solution)/shard_map/ppermute | solution.py:91
  82.4 6.4 %collective-permute-start.2 = (bf16[512,1,128]{0,2,1:T(8,128)(2,1)S(1)}, bf16[512,1,128]{0,2,1:T(8,128)(2,1)S(1)}, u32[]{:S(2)}, u32[]{:S(2)}) collective-permute-start(bf16[512,1,128]{0,2,1:T(8,128)(2,1)S(1)} %collective-permute-done.1), channel_id=1, source_target_pairs={{0,16},{16,32},{32,48},{48,64},{64,80},{80,96},{96,112},{112,0},{1... | collective-permute-start | bytes 393224 | tf_op jit(solution)/shard_map/ppermute | solution.py:91
  85.1 8.3 %collective-permute-start.5 = (bf16[512,1,128]{0,2,1:T(8,128)(2,1)S(1)}, bf16[512,1,128]{0,2,1:T(8,128)(2,1)S(1)}, u32[]{:S(2)}, u32[]{:S(2)}) collective-permute-start(bf16[512,1,128]{0,2,1:T(8,128)(2,1)S(1)} %collective-permute-done.4), channel_id=1, source_target_pairs={{0,112},{16,0},{32,16},{48,32},{64,48},{80,64},{96,80},{112,96},{1... | collective-permute-start | bytes 393224 | tf_op jit(solution)/shard_map/ppermute | solution.py:94
  88.8 7.2 %collective-permute-start.3 = (bf16[512,1,128]{0,2,1:T(8,128)(2,1)S(1)}, bf16[512,1,128]{0,2,1:T(8,128)(2,1)S(1)}, u32[]{:S(2)}, u32[]{:S(2)}) collective-permute-start(bf16[512,1,128]{0,2,1:T(8,128)(2,1)S(1)} %collective-permute-done.2), channel_id=1, source_target_pairs={{0,16},{16,32},{32,48},{48,64},{64,80},{80,96},{96,112},{112,0},{1... | collective-permute-start | bytes 393224 | tf_op jit(solution)/shard_map/ppermute | solution.py:91
  93.4 8.2 %collective-permute-start.6 = (bf16[512,1,128]{0,2,1:T(8,128)(2,1)S(1)}, bf16[512,1,128]{0,2,1:T(8,128)(2,1)S(1)}, u32[]{:S(2)}, u32[]{:S(2)}) collective-permute-start(bf16[512,1,128]{0,2,1:T(8,128)(2,1)S(1)} %collective-permute-done.5), channel_id=1, source_target_pairs={{0,112},{16,0},{32,16},{48,32},{64,48},{80,64},{96,80},{112,96},{1... | collective-permute-start | bytes 393224 | tf_op jit(solution)/shard_map/ppermute | solution.py:94
  108.7 9.1 %copy-start.6 = (bf16[512,1,2,128]{3,0,2,1:T(8,128)(2,1)S(1)}, bf16[512,1,2,128]{3,0,2,1:T(8,128)(2,1)}, u32[]{:S(2)}) copy-start(bf16[512,1,2,128]{3,0,2,1:T(8,128)(2,1)} %get-tuple-element.122) | copy-start | bytes 786436 | tf_op jit(solution)/shard_map/cond
  117.8 5.5 %copy-start.3 = (pred[512,4096]{0,1:T(8,128)(4,1)S(1)}, pred[512,4096]{0,1:T(8,128)(4,1)}, u32[]{:S(2)}) copy-start(pred[512,4096]{0,1:T(8,128)(4,1)} %compare_and_fusion) | copy-start | bytes 6291460 | tf_op jit(solution)/shard_map/cond
  117.8 5.5 %copy-start.12 = (bf16[4096,1,128]{2,0,1:T(8,128)(2,1)S(1)}, bf16[4096,1,128]{2,0,1:T(8,128)(2,1)}, u32[]{:S(2)}) copy-start(bf16[4096,1,128]{2,0,1:T(8,128)(2,1)} %get-tuple-element.123) | copy-start | bytes 3145732 | tf_op jit(solution)/shard_map/cond
  138.1 74.6 %copy-start.4 = (bf16[32,5376]{1,0:T(8,128)(2,1)S(1)}, bf16[32,5376]{1,0:T(8,128)(2,1)}, u32[]{:S(2)}) copy-start(bf16[32,5376]{1,0:T(8,128)(2,1)} %param.12) | copy-start | bytes 1032196
  138.1 74.7 %copy-start.7 = (f32[5376]{0:T(1024)S(1)}, f32[5376]{0:T(1024)}, u32[]{:S(2)}) copy-start(f32[5376]{0:T(1024)} %param.21) | copy-start | bytes 64516
Sparse Core Ops, SparseCore 0:
  9.2 45.2 all-gather.3
  68.3 38.3 all-gather.5
  138.2 73.2 reduce-scatter.1
